TPU v7x, 32 devices: a whole 2x2x4 slice. The times are simulated.
32 devices in a mesh: chan: 8 (over y, x, core), win: 4 (over z).
Axes of the slice: x: 2, y: 2, z: 4, core: 2. Of those that a mesh axis runs over, the one named last changes fastest.
Arguments:
- spectra: float32 [4, 256, 2, 4096], P('win', 'chan'), may hold values from -2000 to 2000
- sources: int32 [2, 8], replicated, may hold values from 0 to 255, as said below
- window_valid: int32 [4, 256], P('win', 'chan'), may hold values 0 or 1
Outputs:
- correlations: float32 [2, 8, 256, 256], P(None, 'win', 'chan')
Inputs may be any that keep to these rules, and one draw needn't show every extreme that they name: sources[t, s] is a channel of owner s, that is between (s) * 32 and (s + 1) * 32 - 1; the entries of one turn are distinct.
All inputs are finite; a program needn't handle non-finite values. No bound on the sum of `window_valid` on one device may be relied on, other than what follows from the above.
Results may differ from a plain program's by a relative error of at most 0.0022.
Values may be sent and summed in bfloat16 or wider, within the bound.
A program may use at most 64 MiB of HBM per device.

v0:
```python
import math

import jax
import jax.numpy as jnp
from jax import lax
from jax.sharding import PartitionSpec as P

LAGS = 256


def whiten(spectra, window_valid):
    mean_power = jnp.mean(spectra * spectra, axis=(2, 3), keepdims=True)
    valid_flags = window_valid.astype(jnp.float32)[:, :, None, None]
    whitened = valid_flags * spectra / jnp.sqrt(mean_power + 1e-05)
    return whitened.astype(jnp.bfloat16).reshape(
        spectra.shape[0], spectra.shape[1], 2 * spectra.shape[3]
    )


def build_table(freq_count, lag_count):
    shifts = jnp.arange(lag_count, dtype=jnp.int32) - lag_count // 2
    freq_bins = jnp.arange(freq_count, dtype=jnp.int32)
    phase_index = freq_bins[:, None] * shifts[None, :] % (2 * freq_count)
    angles = phase_index.astype(jnp.float32) * (math.pi / freq_count)
    return jnp.concatenate([jnp.cos(angles), -jnp.sin(angles)], axis=0).astype(jnp.bfloat16)


def cross_block(source_piece, receivers, trig_table):
    half_width = receivers.shape[2] // 2
    src_real = source_piece[:, :, None, :half_width].astype(jnp.float32)
    src_imag = source_piece[:, :, None, half_width:].astype(jnp.float32)
    rec_real = receivers[:, None, :, :half_width].astype(jnp.float32)
    rec_imag = receivers[:, None, :, half_width:].astype(jnp.float32)
    cross_real = (src_real * rec_real + src_imag * rec_imag).astype(jnp.bfloat16)
    cross_imag = (src_imag * rec_real - src_real * rec_imag).astype(jnp.bfloat16)
    cross_both = jnp.concatenate([cross_real, cross_imag], axis=-1)
    lag_values = jnp.dot(
        cross_both.reshape(-1, 2 * half_width), trig_table, preferred_element_type=jnp.float32
    )
    lag_values = lag_values.reshape(
        source_piece.shape[0], source_piece.shape[1], receivers.shape[1], -1
    )
    return jnp.sum(lag_values, axis=0)


def local(spectra, sources, window_valid):
    whitened = whiten(spectra, window_valid)
    win_local = whitened.shape[0]
    chan_local = whitened.shape[1]
    freq_count = spectra.shape[3]
    turn_count = sources.shape[0]
    trig_table = build_table(freq_count, LAGS)
    norm_scale = 1.0 / math.sqrt(freq_count * win_local * lax.axis_size("win"))
    own_count = sources.shape[1] // lax.axis_size("chan")
    owner_index = lax.axis_index("chan")
    local_rows = (
        lax.dynamic_slice_in_dim(sources, owner_index * own_count, own_count, 1)
        - owner_index * chan_local
    )
    picked = jnp.take(whitened, local_rows.reshape(-1), axis=1).reshape(
        win_local, turn_count, own_count, 2 * freq_count
    )
    everything = lax.all_gather(picked, "chan", axis=2, tiled=True)
    per_turn = [everything[:, turn_index] for turn_index in range(turn_count)]
    results = []
    for gathered in per_turn:
        share_rows = gathered.shape[1] // lax.axis_size("win")

        def stack_term(first_row, row_count, gathered=gathered):
            sub_size = math.gcd(row_count, 8)
            sub_number = row_count // sub_size
            sub_blocks = gathered.reshape(
                win_local, sub_number, sub_size, 2 * freq_count
            ).transpose(1, 0, 2, 3)
            partial_value = lax.map(
                lambda source_piece: cross_block(source_piece, whitened, trig_table), sub_blocks
            )
            return partial_value.reshape(row_count, chan_local, -1)

        stacked = lax.psum_scatter(
            stack_term(jnp.int32(0), share_rows * lax.axis_size("win")),
            "win",
            scatter_dimension=0,
            tiled=True,
        )
        results.append(stacked * norm_scale)
    return jnp.stack(results, axis=0)


def solution(mesh):
    placed = (P("win", "chan", None, None), P(), P("win", "chan"))
    return jax.shard_map(
        local, mesh=mesh, in_specs=placed, out_specs=P(None, "win", "chan", None), check_vma=False
    )
```

profile of v0, /device:TPU:0, one launch (start us, length us, event | category | flops | bytes accessed | tf_op | source)
XLA Modules:
  0.0 96.3 jit_solution(6179811309796717721)
XLA Ops:
  6.5 0.0 reduce-scatter.3.cloned.1.call-start
  6.5 0.9 and_reduce_fusion
  7.4 0.1 reduce.2
  7.5 1.9 %multiply_reduce_fusion = f32[32]{0:T(128)S(1)} fusion(f32[1,32,2,4096]{3,2,1,0:T(2,128)} %param.3), kind=kLoop, calls=%fused_computation.25 | loop fusion | flops 524256 | bytes 1048704 | tf_op jit(solution)/shard_map/reduce_sum | solution.py:12
  9.4 0.7 convert_bitcast_fusion
  10.1 1.9 %fusion.12 = bf16[1,32,2,4096]{3,2,1,0:T(2,128)(2,1)S(1)} fusion(f32[1,32,2,4096]{3,2,1,0:T(2,128)} %param.3, f32[32]{0:T(128)S(1)} %add_sqrt_fusion, f32[32]{0:T(128)S(1)} %convert_bitcast_fusion), kind=kLoop, calls=%fused_computation.27 | loop fusion | flops 786432 | bytes 1573120 | tf_op jit(solution)/shard_map/convert_element_type | solution.py:15
  12.0 0.4 reshape.261
  12.4 0.3 copy.9
  12.7 0.6 gather_fusion
  13.3 0.1 fusion.19
  13.4 10.8 %all_gather.3 = bf16[1,2,8,8192]{3,1,0,2:T(2,128)(2,1)S(1)} all-gather(bf16[1,2,1,8192]{3,1,0,2:T(2,128)(2,1)S(1)} %fusion.19), channel_id=1, replica_groups=mesh['chan'=8,'win'=4] {'chan'}, dimensions={2}, use_global_device_ids=true | all-gather | bytes 294912 | tf_op jit(solution)/shard_map/all_gather | solution.py:63
  24.2 0.5 fusion.22
  24.6 0.3 copy_bitcast_fusion
  25.0 0.1 fusion.14
  25.1 17.0 %cosine_convert_fusion = (bf16[4096,256]{1,0:T(8,128)(2,1)S(1)}, bf16[4096,256]{1,0:T(8,128)(2,1)S(1)}) fusion(s32[256]{0:T(256)S(1)} %iota_add_fusion), kind=kLoop, calls=%fused_computation.19 | loop fusion | flops 17825792 | bytes 4195328 | tf_op jit(solution)/shard_map/convert.6
  42.0 0.0 copy-start
  42.1 0.0 copy-start.1
  42.1 3.5 %add_convert_fusion.1 = (bf16[1,8,32,4096]{3,2,1,0:T(8,128)(2,1)S(1)}, bf16[1,8,32,4096]{3,2,1,0:T(8,128)(2,1)S(1)}, bf16[1,8,32,4096]{3,2,1,0:T(8,128)(2,1)S(1)}, bf16[1,8,32,4096]{3,2,1,0:T(8,128)(2,1)}) fusion(f32[32,4096]{1,0:T(8,128)S(1)} %get-tuple-element.44, f32[8,4096]{1,0:T(8,128)S(1)} %get-tuple-element.48, f32[32,4096]{1,0:T(8,128)S(1)} %get-tuple-element.42, ...), kind=kLoop, calls=%fused_computation.23 | loop fusion | flops 16777216 | bytes 9961472 | tf_op jit(solution)/shard_map/while/body/eval_jaxpr/convert_element_type | solution.py:34
  45.6 0.0 copy-done
  45.6 0.0 copy-done.1
  45.6 1.9 %fusion.3 = f32[8,32,256]{2,1,0:T(8,128)} fusion(bf16[1,8,32,4096]{3,2,1,0:T(8,128)(2,1)S(1)} %get-tuple-element.31, bf16[1,8,32,4096]{3,2,1,0:T(8,128)(2,1)S(1)} %get-tuple-element.30, bf16[4096,256]{1,0:T(8,128)(2,1)S(1)} %get-tuple-element.52, bf16[4096,256]{1,0:T(8,128)(2,1)S(1)} %get-tuple-element.51), kind=kOutput, calls=%fused_computation.8 | convolution fusion | flops 1090519040 | bytes 8650752 | tf_op jit(solution)/shard_map/while/body/eval_jaxpr/dot_general | solution.py:37
  47.5 0.0 reduce-scatter.3.cloned.1.call-update
  47.6 0.0 reduce-scatter.5.cloned.1.call-start
  47.6 4.8 %fusion.6 = f32[8,32,256]{2,1,0:T(8,128)} fusion(bf16[1,8,32,4096]{3,2,1,0:T(8,128)(2,1)S(1)} %get-tuple-element.34, bf16[1,8,32,4096]{3,2,1,0:T(8,128)(2,1)} %get-tuple-element.40, bf16[4096,256]{1,0:T(8,128)(2,1)} %copy-done.1, bf16[4096,256]{1,0:T(8,128)(2,1)} %copy-done), kind=kOutput, calls=%fused_computation.13 | convolution fusion | flops 1090519040 | bytes 8650752 | tf_op jit(solution)/shard_map/while/body/eval_jaxpr/dot_general | solution.py:37
  52.4 0.0 reduce-scatter.5.cloned.1.call-update
  52.5 15.2 %reduce-scatter.3.cloned.1.call-done = f32[2,32,256]{2,1,0:T(8,128)} async-done(((f32[8,32,256]{2,1,0:T(8,128)}), f32[2,32,256]{2,1,0:T(8,128)}) %reduce-scatter.3.cloned.1.call-update) | async-done | bytes 65552 | tf_op jit(solution)/shard_map/reduce_scatter | solution.py:80
  67.6 0.8 multiply_bitcast_fusion.1
  68.5 19.5 %reduce-scatter.5.cloned.1.call-done = f32[2,32,256]{2,1,0:T(8,128)} async-done(((f32[8,32,256]{2,1,0:T(8,128)}), f32[2,32,256]{2,1,0:T(8,128)}) %reduce-scatter.5.cloned.1.call-update) | async-done | bytes 65552 | tf_op jit(solution)/shard_map/reduce_scatter | solution.py:80
  87.9 0.8 multiply_bitcast_fusion
  88.8 0.7 pad_maximum_fusion
  (5 shorter events, 0.1 us)
Async XLA Ops:
  6.5 61.1 %reduce-scatter.3.cloned.1.call-start = ((), (), s32[]{:S(2)}) async-start(), calls=%async_computation.2 | async-start | bytes 327680 | tf_op jit(solution)/shard_map/reduce_scatter | solution.py:80
  42.0 3.5 %copy-start = (bf16[4096,256]{1,0:T(8,128)(2,1)}, bf16[4096,256]{1,0:T(8,128)(2,1)S(1)}, u32[]{:S(2)}) copy-start(bf16[4096,256]{1,0:T(8,128)(2,1)S(1)} %get-tuple-element.51) | copy-start | bytes 6291460
  42.1 3.5 %copy-start.1 = (bf16[4096,256]{1,0:T(8,128)(2,1)}, bf16[4096,256]{1,0:T(8,128)(2,1)S(1)}, u32[]{:S(2)}) copy-start(bf16[4096,256]{1,0:T(8,128)(2,1)S(1)} %get-tuple-element.52) | copy-start | bytes 6291460
  47.6 40.4 %reduce-scatter.5.cloned.1.call-start = ((), (), s32[]{:S(2)}) async-start(), calls=%async_computation.3 | async-start | bytes 327680 | tf_op jit(solution)/shard_map/reduce_scatter | solution.py:80
Sparse Core Ops, SparseCore 0:
  47.7 19.8 reduce-scatter.2
  70.0 17.9 reduce-scatter.4
where the time goes:
time: 96.6 us; the launch traced here: 96.3 us
  waiting for transfers between devices  34.7 us (36%)
  other arithmetic  28.5 us (30%)
  between operations  13.5 us (14%)
  blocking collectives  10.8 us (11%)
  matrix products  6.77 us (7%)
  local copies, waits for them, and re-layouts  2.06 us (2%)
    reduce_scatter x2, waiting for transfers between devices, local(): lax.psum_scatter(stack_term(jnp.int32(0), share_rows * lax.axis_size('win...  34.6 us
    another operation x1, other arithmetic  17 us
    all_gather x1, blocking collectives, local(): everything = lax.all_gather(picked, 'chan', axis=2, tiled=True)  10.8 us
    dot_general x2, matrix products, cross_block(): jnp.dot(cross_both.reshape(-1, 2 * half_width), trig_table, preferred_ele...  6.77 us
    convert_element_type x1, other arithmetic, cross_block(): (src_real * rec_real + src_imag * rec_imag).astype(jnp.bfloat16)  3.51 us
    another operation x3, other arithmetic, local(): return jnp.stack(results, axis=0)  2.35 us
  transfers between devices with their start and end apart: 2, of which 2 were waited for; matrix products, arithmetic and copies ran while one was open for 6% of the time, Pallas kernels for 0%

commit v1 on v0

v1 whole, which is shorter than its diff:
```python
import functools
import math

import jax
import jax.numpy as jnp
import ml_dtypes
import numpy as np
from jax import lax
from jax.experimental import pallas as pl
from jax.experimental.pallas import tpu as pltpu
from jax.sharding import PartitionSpec as P

LAGS = 256
LANES = 128
CHUNK = 256
MESH = pl.DeviceIdType.MESH


def build_table(freq_count, lag_count):
    shifts = np.arange(lag_count, dtype=np.int64) - lag_count // 2
    freq_bins = np.arange(freq_count, dtype=np.int64)
    phase_index = (freq_bins[:, None] * shifts[None, :]) % (2 * freq_count)
    angles = phase_index.astype(np.float32) * np.float32(math.pi / freq_count)
    table = np.stack([np.cos(angles), -np.sin(angles)]).astype(ml_dtypes.bfloat16)
    table = table.reshape(2, freq_count // CHUNK, CHUNK, lag_count).transpose(1, 0, 2, 3)
    return np.ascontiguousarray(table.reshape(freq_count // CHUNK, 2 * CHUNK, lag_count))


def kernel(
    chan_size, win_size, turns, spec_hbm, trig_hbm, valid_ref, sources_ref, out_ref,
    spec, trig, real, imag, gathered, srcs, sent, kept, received, acc,
    local_sem, gather_send, gather_recv, stack_send, stack_recv,
):
    chan_local = valid_ref.shape[1]
    rows = spec.shape[0] // chan_local
    me_c, me_w = lax.axis_index("chan"), lax.axis_index("win")
    share = chan_size // win_size
    wins_half = win_size // 2
    per_half = share * wins_half
    group = math.gcd(per_half, 4)

    spec_copy = pltpu.make_async_copy(spec_hbm, spec, local_sem.at[0])
    spec_copy.start()
    trig_copy = pltpu.make_async_copy(trig_hbm, trig, local_sem.at[1])
    trig_copy.start()
    barrier = pltpu.get_barrier_semaphore()
    for d in range(1, chan_size):
        pl.semaphore_signal(
            barrier, inc=1, device_id={"chan": lax.rem(me_c + d, chan_size)}, device_id_type=MESH
        )
    for d in range(1, win_size):
        pl.semaphore_signal(
            barrier, inc=1, device_id={"win": lax.rem(me_w + d, win_size)}, device_id_type=MESH
        )
    valid = valid_ref[...].astype(jnp.float32)
    lane = lax.broadcasted_iota(jnp.int32, (1, chan_local), 1)
    inverse = 1.0 / (rows * LANES)
    spec_copy.wait()

    for t in range(turns):
        row = jnp.full((1, LANES), sources_ref[t, me_c] - me_c * chan_local, jnp.int32)
        wanted = jnp.broadcast_to(row, (rows, LANES))
        picked = jnp.zeros((rows, LANES), jnp.float32)
        for c in range(chan_local):
            picked = jnp.where(wanted == c, spec[c * rows:(c + 1) * rows, :], picked)
        power = jnp.sum(jnp.sum(picked * picked, axis=0, keepdims=True), axis=1, keepdims=True)
        flag = jnp.sum(jnp.where(lane == row[:, :chan_local], valid, 0.0), axis=1, keepdims=True)
        scale = flag / jnp.sqrt(power * inverse + 1e-05)
        gathered[me_c, t * rows:(t + 1) * rows, :] = (picked * scale).astype(jnp.bfloat16)

    pl.semaphore_wait(barrier, chan_size - 1 + win_size - 1)

    def gather_copy(peer, owner):
        return pltpu.make_async_remote_copy(
            src_ref=gathered.at[owner],
            dst_ref=gathered.at[owner],
            send_sem=gather_send.at[peer],
            recv_sem=gather_recv.at[owner],
            device_id={"chan": peer},
            device_id_type=MESH,
        )

    for d in range(chan_size - 1, 0, -1):
        gather_copy(lax.rem(me_c + d, chan_size), me_c).start()

    squares = jnp.zeros((chan_local, LANES), jnp.float32)
    for i in range(rows):
        value = spec[pl.ds(i, chan_local, stride=rows), :]
        squares = squares + value * value
    power = jnp.sum(squares, axis=1, keepdims=True)
    across = lax.broadcasted_iota(jnp.int32, (chan_local, chan_local), 0)
    along = lax.broadcasted_iota(jnp.int32, (chan_local, chan_local), 1)
    flags = jnp.sum(jnp.where(across == along, valid, 0.0), axis=1, keepdims=True)
    scale = flags / jnp.sqrt(power * inverse + 1e-05)
    scale = jnp.broadcast_to(scale, (chan_local, LANES))
    for i in range(rows):
        value = spec[pl.ds(i, chan_local, stride=rows), :] * scale
        part = imag if i % 2 else real
        lanes = slice(i // 2 * LANES, i // 2 * LANES + LANES)
        part[:, lanes] = value.astype(jnp.bfloat16).astype(jnp.float32)
    trig_copy.wait()

    def stack_copy(target, origin):
        return pltpu.make_async_remote_copy(
            src_ref=sent.at[pl.ds(target * share, share)],
            dst_ref=received.at[origin],
            send_sem=stack_send.at[target],
            recv_sem=stack_recv.at[origin],
            device_id={"win": target},
            device_id_type=MESH,
        )

    my_half = me_w // wins_half
    for phase in range(2):
        half = my_half if phase else 1 - my_half
        first = half * per_half

        def arrive(i, carry, first=first):
            owner = first + i

            @pl.when(owner != me_c)
            def _():
                gather_copy(me_c, owner).wait_recv()

            srcs[owner] = gathered[owner].astype(jnp.float32)
            return carry

        lax.fori_loop(0, per_half, arrive, 0)

        def block(b, carry, first=first, phase=phase):
            slot = first + b * group
            acc[...] = jnp.zeros_like(acc)

            def step(k, inner):
                bins = pl.ds(pl.multiple_of(k * CHUNK, CHUNK), CHUNK)
                x, y = real[:, bins], imag[:, bins]
                reals, imags = [], []
                for i in range(group):
                    for t in range(turns):
                        base = t * rows + k * (2 * CHUNK // LANES)
                        pieces = [
                            srcs[slot + i, pl.ds(base + j, 1), :] for j in range(2 * CHUNK // LANES)
                        ]
                        a = jnp.concatenate(pieces[0::2], axis=1)
                        b_ = jnp.concatenate(pieces[1::2], axis=1)
                        reals.append((a * x + b_ * y).astype(jnp.bfloat16))
                        imags.append((b_ * x - a * y).astype(jnp.bfloat16))
                cross = jnp.concatenate(
                    [jnp.concatenate(reals, axis=0), jnp.concatenate(imags, axis=0)], axis=1
                )
                acc[...] += jnp.dot(cross, trig[k], preferred_element_type=jnp.float32)
                return inner

            lax.fori_loop(0, real.shape[1] // CHUNK, step, 0, unroll=2)
            for i in range(group):
                for t in range(turns):
                    at = (i * turns + t) * chan_local
                    value = acc[at:at + chan_local, :]
                    sent[slot + i, t] = value.astype(jnp.bfloat16)
                    if phase:
                        kept[b * group + i, t] = value
            return carry

        if per_half == group:
            block(0, 0)
        else:
            lax.fori_loop(0, per_half // group, block, 0)
        for i in range(wins_half):
            target = half * wins_half + i
            if phase == 0:
                stack_copy(target, me_w).start()
            else:

                @pl.when(target != me_w)
                def _(target=target):
                    stack_copy(target, me_w).start()

    base = lax.rem(me_w, wins_half) * share
    others = [lax.rem(me_w + d, win_size) for d in range(1, win_size)]
    for other in others:
        stack_copy(me_w, other).wait_recv()
    for j in range(share):
        for t in range(turns):
            total = kept[base + j, t]
            for other in others:
                total = total + received[other, j, t].astype(jnp.float32)
            out_ref[t, j] = total
    for d in range(1, chan_size):
        gather_copy(lax.rem(me_c + d, chan_size), me_c).wait_send()
    for other in others:
        stack_copy(other, me_w).wait_send()


def local(spectra, sources, window_valid):
    chan_size, win_size = lax.axis_size("chan"), lax.axis_size("win")
    win_local, chan_local, _, freq_count = spectra.shape
    turns, slots = sources.shape
    assert win_local == 1 and slots == chan_size and chan_size % win_size == 0
    blocks = freq_count // LANES
    rows = 2 * blocks
    share = slots // win_size
    per_half = slots // 2
    group = math.gcd(per_half, 4)
    spread = spectra.reshape(chan_local, 2, blocks, LANES).transpose(0, 2, 1, 3)
    spread = spread.reshape(chan_local * rows, LANES)
    table = jnp.asarray(build_table(freq_count, LAGS))
    norm_scale = 1.0 / math.sqrt(freq_count * win_local * win_size)
    stacked = pl.pallas_call(
        functools.partial(kernel, chan_size, win_size, turns),
        out_shape=jax.ShapeDtypeStruct((turns, share, chan_local, LAGS), jnp.float32),
        in_specs=[
            pl.BlockSpec(memory_space=pltpu.HBM),
            pl.BlockSpec(memory_space=pltpu.HBM),
            pl.BlockSpec(memory_space=pltpu.VMEM),
            pl.BlockSpec(memory_space=pltpu.SMEM),
        ],
        out_specs=pl.BlockSpec(memory_space=pltpu.VMEM),
        scratch_shapes=[
            pltpu.VMEM((chan_local * rows, LANES), jnp.float32),
            pltpu.VMEM(table.shape, jnp.bfloat16),
            pltpu.VMEM((chan_local, freq_count), jnp.float32),
            pltpu.VMEM((chan_local, freq_count), jnp.float32),
            pltpu.VMEM((slots, turns * rows, LANES), jnp.bfloat16),
            pltpu.VMEM((slots, turns * rows, LANES), jnp.float32),
            pltpu.VMEM((slots, turns, chan_local, LAGS), jnp.bfloat16),
            pltpu.VMEM((per_half, turns, chan_local, LAGS), jnp.float32),
            pltpu.VMEM((win_size, share, turns, chan_local, LAGS), jnp.bfloat16),
            pltpu.VMEM((group * turns * chan_local, LAGS), jnp.float32),
            pltpu.SemaphoreType.DMA((2,)),
            pltpu.SemaphoreType.DMA((chan_size,)),
            pltpu.SemaphoreType.DMA((chan_size,)),
            pltpu.SemaphoreType.DMA((win_size,)),
            pltpu.SemaphoreType.DMA((win_size,)),
        ],
        compiler_params=pltpu.CompilerParams(
            collective_id=0, has_side_effects=True, vmem_limit_bytes=63 * 1024 * 1024
        ),
        cost_estimate=pl.CostEstimate(
            flops=2 * turns * slots * chan_local * 2 * freq_count * LAGS,
            bytes_accessed=8 * 1024 * 1024,
            transcendentals=0,
        ),
    )(spread, table, window_valid, sources)
    return stacked * norm_scale


def solution(mesh):
    placed = (P("win", "chan", None, None), P(), P("win", "chan"))
    return jax.shard_map(
        local, mesh=mesh, in_specs=placed, out_specs=P(None, "win", "chan", None), check_vma=False
    )
```

time: 96.6 us -> 22.4 us (0.23)
  waiting for transfers between devices: 34.7 us -> 0 us
  other arithmetic: 28.5 us -> 1.57 us
  Pallas kernels: 0 us -> 20.7 us
  between operations: 13.5 us -> 0.01 us
  blocking collectives: 10.8 us -> 0 us
  matrix products: 6.77 us -> 0 us
  local copies, waits for them, and re-layouts: 2.06 us -> 0 us
    reduce_scatter x2 -> x0, waiting for transfers between devices: 34.6 us -> none  [local(): lax.psum_scatter(stack_term(jnp.int32(0), share_rows * lax.axis_size('win...]
    pallas_call x0 -> x1, Pallas kernels: none -> 20.7 us  [local(): pl.pallas_call(functools.partial(kernel, chan_size, win_size, turns), out...]
    another operation x4 -> x0, other arithmetic: 19.3 us -> none
    all_gather x1 -> x0, blocking collectives: 10.8 us -> none  [local(): everything = lax.all_gather(picked, 'chan', axis=2, tiled=True)]
    dot_general x2 -> x0, matrix products: 6.77 us -> none  [cross_block(): jnp.dot(cross_both.reshape(-1, 2 * half_width), trig_table, preferred_ele...]
    convert_element_type x5 -> x0, other arithmetic: 5.51 us -> none  [the longest x1 3.51 us: cross_block(): (src_real * rec_real + src_imag * rec_imag).astype(jnp.bfloat16)]
    reduce_sum x1 -> x0, other arithmetic: 1.88 us -> none  [whiten(): mean_power = jnp.mean(spectra * spectra, axis=(2, 3), keepdims=True)]
  transfers between devices with their start and end apart: 2 -> 0, of which waited for: 2 -> 0; matrix products, arithmetic and copies ran while one was open for 6% -> 0% of each run, Pallas kernels for 0% -> 0%
where the time goes in v1:
time: 22.4 us; the launch traced here: 22.3 us
  Pallas kernels  20.7 us (92%)
  other arithmetic  1.57 us (7%)
    pallas_call x1, Pallas kernels, local(): pl.pallas_call(functools.partial(kernel, chan_size, win_size, turns), out...  20.7 us
    mul x1, other arithmetic, local(): return stacked * norm_scale  1.57 us

profile of v1, /device:TPU:0, one launch (start us, length us, event | category | flops | bytes accessed | tf_op | source)
XLA Modules:
  0.0 22.3 jit_solution(552952360461367398)
XLA Ops:
  0.0 20.7 %shard_map.46 = f32[2,2,32,256]{3,2,1,0:T(8,128)} custom-call(f32[2048,128]{1,0:T(8,128)} %bitcast.5, bf16[16,512,256]{2,1,0:T(8,128)(2,1)} %constant.4.clone.trig_hbm, s32[1,32]{1,0:T(1,128)} %valid_ref.1, s32[2,8]{1,0:T(2,128)} %sources_ref.1), custom_call_target="tpu_custom_call" | custom-call | flops 2147483648 | bytes 8388608 | tf_op jit(solution)/shard_map/pallas_call | solution.py:208
  20.7 1.6 %broadcast_multiply_fusion = f32[2,2,32,256]{3,2,1,0:T(8,128)} fusion(f32[2,2,32,256]{3,2,1,0:T(8,128)} %shard_map.46), kind=kLoop, calls=%fused_computation | loop fusion | flops 32768 | bytes 262144 | tf_op jit(solution)/shard_map/mul | solution.py:244

commit v2 on v1

--- a/solution.py
+++ b/solution.py
@@ -27,8 +27,8 @@
 
 
 def kernel(
-    chan_size, win_size, turns, spec_hbm, trig_hbm, valid_ref, sources_ref, out_ref,
-    spec, trig, real, imag, gathered, srcs, sent, kept, received, acc,
+    chan_size, win_size, turns, spec_hbm, trig_hbm, valid_hbm, sources_hbm, out_ref,
+    spec, trig, valid_ref, sources_ref, real, imag, gathered, srcs, sent, kept, received, acc,
     local_sem, gather_send, gather_recv, stack_send, stack_recv,
 ):
     chan_local = valid_ref.shape[1]
@@ -39,19 +39,25 @@
     per_half = share * wins_half
     group = math.gcd(per_half, 4)
 
+    barrier = pltpu.get_barrier_semaphore()
+    for d in range(1, win_size):
+        pl.semaphore_signal(
+            barrier, inc=1, device_id={"win": lax.rem(me_w + d, win_size)}, device_id_type=MESH
+        )
+    for d in range(1, chan_size):
+        pl.semaphore_signal(
+            barrier, inc=1, device_id={"chan": lax.rem(me_c + d, chan_size)}, device_id_type=MESH
+        )
+    sources_copy = pltpu.make_async_copy(sources_hbm, sources_ref, local_sem.at[2])
+    sources_copy.start()
+    valid_copy = pltpu.make_async_copy(valid_hbm, valid_ref, local_sem.at[3])
+    valid_copy.start()
     spec_copy = pltpu.make_async_copy(spec_hbm, spec, local_sem.at[0])
     spec_copy.start()
     trig_copy = pltpu.make_async_copy(trig_hbm, trig, local_sem.at[1])
     trig_copy.start()
-    barrier = pltpu.get_barrier_semaphore()
-    for d in range(1, chan_size):
-        pl.semaphore_signal(
-            barrier, inc=1, device_id={"chan": lax.rem(me_c + d, chan_size)}, device_id_type=MESH
-        )
-    for d in range(1, win_size):
-        pl.semaphore_signal(
-            barrier, inc=1, device_id={"win": lax.rem(me_w + d, win_size)}, device_id_type=MESH
-        )
+    sources_copy.wait()
+    valid_copy.wait()
     valid = valid_ref[...].astype(jnp.float32)
     lane = lax.broadcasted_iota(jnp.int32, (1, chan_local), 1)
     inverse = 1.0 / (rows * LANES)
@@ -151,7 +157,7 @@
                 acc[...] += jnp.dot(cross, trig[k], preferred_element_type=jnp.float32)
                 return inner
 
-            lax.fori_loop(0, real.shape[1] // CHUNK, step, 0, unroll=2)
+            lax.fori_loop(0, real.shape[1] // CHUNK, step, 0, unroll=8)
             for i in range(group):
                 for t in range(turns):
                     at = (i * turns + t) * chan_local
@@ -211,13 +217,15 @@
         in_specs=[
             pl.BlockSpec(memory_space=pltpu.HBM),
             pl.BlockSpec(memory_space=pltpu.HBM),
-            pl.BlockSpec(memory_space=pltpu.VMEM),
-            pl.BlockSpec(memory_space=pltpu.SMEM),
+            pl.BlockSpec(memory_space=pltpu.HBM),
+            pl.BlockSpec(memory_space=pltpu.HBM),
         ],
         out_specs=pl.BlockSpec(memory_space=pltpu.VMEM),
         scratch_shapes=[
             pltpu.VMEM((chan_local * rows, LANES), jnp.float32),
             pltpu.VMEM(table.shape, jnp.bfloat16),
+            pltpu.VMEM(window_valid.shape, jnp.int32),
+            pltpu.SMEM(sources.shape, jnp.int32),
             pltpu.VMEM((chan_local, freq_count), jnp.float32),
             pltpu.VMEM((chan_local, freq_count), jnp.float32),
             pltpu.VMEM((slots, turns * rows, LANES), jnp.bfloat16),
@@ -226,7 +234,7 @@
             pltpu.VMEM((per_half, turns, chan_local, LAGS), jnp.float32),
             pltpu.VMEM((win_size, share, turns, chan_local, LAGS), jnp.bfloat16),
             pltpu.VMEM((group * turns * chan_local, LAGS), jnp.float32),
-            pltpu.SemaphoreType.DMA((2,)),
+            pltpu.SemaphoreType.DMA((4,)),
             pltpu.SemaphoreType.DMA((chan_size,)),
             pltpu.SemaphoreType.DMA((chan_size,)),
             pltpu.SemaphoreType.DMA((win_size,)),

time: 22.4 us -> 19.8 us (0.88)
  Pallas kernels: 20.7 us -> 18.1 us
    pallas_call x1, Pallas kernels: 20.7 us -> 18.1 us  [local(): pl.pallas_call(functools.partial(kernel, chan_size, win_size, turns), out...]
where the time goes in v2:
time: 19.8 us; the launch traced here: 19.7 us
  Pallas kernels  18.1 us (91%)
  other arithmetic  1.57 us (8%)
    pallas_call x1, Pallas kernels, local(): pl.pallas_call(functools.partial(kernel, chan_size, win_size, turns), out...  18.1 us
    mul x1, other arithmetic, local(): return stacked * norm_scale  1.57 us

profile of v2, /device:TPU:0, one launch (start us, length us, event | category | flops | bytes accessed | tf_op | source)
XLA Modules:
  0.0 19.7 jit_solution(14253799178433152457)
XLA Ops:
  0.0 18.1 %shard_map.46 = f32[2,2,32,256]{3,2,1,0:T(8,128)} custom-call(f32[2048,128]{1,0:T(8,128)} %bitcast.5, bf16[16,512,256]{2,1,0:T(8,128)(2,1)} %constant.4.clone.trig_hbm, s32[1,32]{1,0:T(1,128)} %valid_hbm.1, s32[2,8]{1,0:T(2,128)} %sources_hbm.1), custom_call_target="tpu_custom_call" | custom-call | flops 2147483648 | bytes 8388608 | tf_op jit(solution)/shard_map/pallas_call | solution.py:214
  18.1 1.6 %broadcast_multiply_fusion = f32[2,2,32,256]{3,2,1,0:T(8,128)} fusion(f32[2,2,32,256]{3,2,1,0:T(8,128)} %shard_map.46), kind=kLoop, calls=%fused_computation | loop fusion | flops 32768 | bytes 262144 | tf_op jit(solution)/shard_map/mul | solution.py:252

commit v3 on v2

--- a/solution.py
+++ b/solution.py
@@ -36,8 +36,7 @@
     me_c, me_w = lax.axis_index("chan"), lax.axis_index("win")
     share = chan_size // win_size
     wins_half = win_size // 2
-    per_half = share * wins_half
-    group = math.gcd(per_half, 4)
+    group = math.gcd(share, 4)
 
     barrier = pltpu.get_barrier_semaphore()
     for d in range(1, win_size):
@@ -117,9 +116,12 @@
         )
 
     my_half = me_w // wins_half
-    for phase in range(2):
-        half = my_half if phase else 1 - my_half
-        first = half * per_half
+    targets = [
+        (1 - my_half) * wins_half + lax.rem(me_w + i, wins_half) for i in range(wins_half)
+    ] + [my_half * wins_half + lax.rem(me_w + 1 + i, wins_half) for i in range(wins_half)]
+    for target in targets:
+        mine = target is targets[-1]
+        first = target * share
 
         def arrive(i, carry, first=first):
             owner = first + i
@@ -131,9 +133,9 @@
             srcs[owner] = gathered[owner].astype(jnp.float32)
             return carry
 
-        lax.fori_loop(0, per_half, arrive, 0)
-
-        def block(b, carry, first=first, phase=phase):
+        lax.fori_loop(0, share, arrive, 0)
+
+        def block(b, carry, first=first, mine=mine):
             slot = first + b * group
             acc[...] = jnp.zeros_like(acc)
 
@@ -162,32 +164,25 @@
                 for t in range(turns):
                     at = (i * turns + t) * chan_local
                     value = acc[at:at + chan_local, :]
-                    sent[slot + i, t] = value.astype(jnp.bfloat16)
-                    if phase:
+                    if mine:
                         kept[b * group + i, t] = value
+                    else:
+                        sent[slot + i, t] = value.astype(jnp.bfloat16)
             return carry
 
-        if per_half == group:
+        if share == group:
             block(0, 0)
         else:
-            lax.fori_loop(0, per_half // group, block, 0)
-        for i in range(wins_half):
-            target = half * wins_half + i
-            if phase == 0:
-                stack_copy(target, me_w).start()
-            else:
-
-                @pl.when(target != me_w)
-                def _(target=target):
-                    stack_copy(target, me_w).start()
-
-    base = lax.rem(me_w, wins_half) * share
+            lax.fori_loop(0, share // group, block, 0)
+        if not mine:
+            stack_copy(target, me_w).start()
+
     others = [lax.rem(me_w + d, win_size) for d in range(1, win_size)]
     for other in others:
         stack_copy(me_w, other).wait_recv()
     for j in range(share):
         for t in range(turns):
-            total = kept[base + j, t]
+            total = kept[j, t]
             for other in others:
                 total = total + received[other, j, t].astype(jnp.float32)
             out_ref[t, j] = total
@@ -205,8 +200,7 @@
     blocks = freq_count // LANES
     rows = 2 * blocks
     share = slots // win_size
-    per_half = slots // 2
-    group = math.gcd(per_half, 4)
+    group = math.gcd(share, 4)
     spread = spectra.reshape(chan_local, 2, blocks, LANES).transpose(0, 2, 1, 3)
     spread = spread.reshape(chan_local * rows, LANES)
     table = jnp.asarray(build_table(freq_count, LAGS))
@@ -231,7 +225,7 @@
             pltpu.VMEM((slots, turns * rows, LANES), jnp.bfloat16),
             pltpu.VMEM((slots, turns * rows, LANES), jnp.float32),
             pltpu.VMEM((slots, turns, chan_local, LAGS), jnp.bfloat16),
-            pltpu.VMEM((per_half, turns, chan_local, LAGS), jnp.float32),
+            pltpu.VMEM((share, turns, chan_local, LAGS), jnp.float32),
             pltpu.VMEM((win_size, share, turns, chan_local, LAGS), jnp.bfloat16),
             pltpu.VMEM((group * turns * chan_local, LAGS), jnp.float32),
             pltpu.SemaphoreType.DMA((4,)),

time: 19.8 us -> 19.5 us (0.985)
  Pallas kernels: 18.1 us -> 17.7 us
    pallas_call x1, Pallas kernels: 18.1 us -> 17.7 us  [local(): pl.pallas_call(functools.partial(kernel, chan_size, win_size, turns), out...]
where the time goes in v3:
time: 19.5 us; the launch traced here: 19.3 us
  Pallas kernels  17.7 us (91%)
  other arithmetic  1.57 us (8%)
    pallas_call x1, Pallas kernels, local(): pl.pallas_call(functools.partial(kernel, chan_size, win_size, turns), out...  17.7 us
    mul x1, other arithmetic, local(): return stacked * norm_scale  1.57 us

profile of v3, /device:TPU:0, one launch (start us, length us, event | category | flops | bytes accessed | tf_op | source)
XLA Modules:
  0.0 19.3 jit_solution(16501489179966878203)
XLA Ops:
  0.0 17.7 %shard_map.46 = f32[2,2,32,256]{3,2,1,0:T(8,128)} custom-call(f32[2048,128]{1,0:T(8,128)} %bitcast.5, bf16[16,512,256]{2,1,0:T(8,128)(2,1)} %constant.4.clone.trig_hbm, s32[1,32]{1,0:T(1,128)} %valid_hbm.1, s32[2,8]{1,0:T(2,128)} %sources_hbm.1), custom_call_target="tpu_custom_call" | custom-call | flops 2147483648 | bytes 8388608 | tf_op jit(solution)/shard_map/pallas_call | solution.py:208
  17.7 1.6 %broadcast_multiply_fusion = f32[2,2,32,256]{3,2,1,0:T(8,128)} fusion(f32[2,2,32,256]{3,2,1,0:T(8,128)} %shard_map.46), kind=kLoop, calls=%fused_computation | loop fusion | flops 32768 | bytes 262144 | tf_op jit(solution)/shard_map/mul | solution.py:246
